TPU v7x, 256 devices: a whole 4x4x8 slice. The times are simulated.
256 devices in a mesh: row: 32 (over y_hi, z, core), col: 8 (over x, y_lo).
Axes of the slice: x: 4, y: 4 (y_hi: 2, y_lo: 2; y = y_hi * 2 + y_lo), z: 8, core: 2. Of those that a mesh axis runs over, the one named last changes fastest.
Arguments:
- markers: bfloat16 [32768, 16384], P('row', 'col'), may hold values from -6 to 6
Outputs:
- solved_panel: float32 [1024, 32768], P('col', 'row')
All inputs are finite; a program needn't handle non-finite values.
Results may differ from a plain program's by a relative error of at most 0.00065.
Values may be sent and summed in bfloat16 or wider, within the bound.
A program may use at most 128 MiB of HBM per device.

v0:
```python
import jax
import jax.numpy as jnp
from jax import lax
from jax.sharding import PartitionSpec as P

M = 16384
PANEL = 1024


def add_ridge(gram, row_start, col_start, per_row, rows_dev):
    ranks = row_start + jnp.arange(gram.shape[0], dtype=jnp.int32)
    person = ranks // per_row * rows_dev + ranks % per_row
    columns = col_start + jnp.arange(gram.shape[1], dtype=jnp.int32)
    return gram + jnp.where(person[:, None] == columns[None, :], 0.001, 0.0).astype(jnp.float32)


def lower_inverse(block):
    factor = jnp.linalg.cholesky(block)
    identity = jnp.eye(block.shape[0], dtype=block.dtype)
    return lax.linalg.triangular_solve(factor, identity, left_side=True, lower=True)


def shards(markers):
    rows_dev = markers.shape[0]
    per_row = PANEL // lax.axis_size("row")
    per_col = PANEL // lax.axis_size("col")
    row_index = lax.axis_index("row")
    col_index = lax.axis_index("col")
    panel_local = markers[:per_row]
    partial_gram = lax.dot_general(
        lax.all_gather(panel_local, "row", axis=0, tiled=True),
        markers,
        (((1,), (1,)), ((), ())),
        preferred_element_type=jnp.float32,
    )
    summed = lax.psum_scatter(partial_gram, "col", scatter_dimension=0, tiled=True)
    gram = add_ridge(
        summed * (1.0 / M), col_index * per_col, row_index * rows_dev, per_row, rows_dev
    )
    wide_cols = lax.all_gather(gram[:, :per_row], "row", axis=1, tiled=True)
    diag_block = lax.all_gather(wide_cols, "col", axis=0, tiled=True)
    inverse = lower_inverse(diag_block)
    own_cols = lax.dynamic_slice_in_dim(inverse, col_index * per_col, per_col, 1)
    return lax.psum_scatter(
        jnp.dot(own_cols, gram, precision=lax.Precision.HIGHEST),
        "col",
        scatter_dimension=0,
        tiled=True,
    )


def solution(mesh):
    in_specs = (P("row", "col"),)
    out_specs = P("col", "row")
    return jax.shard_map(shards, mesh=mesh, in_specs=in_specs, out_specs=out_specs, check_vma=False)
```

profile of v0, /device:TPU:1, one launch (start us, length us, event | category | flops | bytes accessed | tf_op | source)
XLA Modules:
  0.0 786.5 jit_solution(4955554423594514966)
XLA Ops:
  8.2 93.1 %all-gather.3.cloned.1.call-done = bf16[1024,2048]{1,0:T(8,128)(2,1)} async-done(((bf16[32,2048]{1,0:T(8,128)(2,1)}), bf16[1024,2048]{1,0:T(8,128)(2,1)}) %all-gather.3.cloned.1.call-update) | async-done | bytes 4194320 | tf_op jit(solution)/shard_map/all_gather | solution.py:31
  101.2 9.9 %fusion.75 = f32[1024,1024]{0,1:T(8,128)} fusion(bf16[1024,2048]{1,0:T(8,128)(2,1)} %all-gather.3.cloned.1.call-done, bf16[1024,2048]{1,0:T(8,128)(2,1)} %param.1), kind=kOutput, calls=%fused_computation.170 | convolution fusion | flops 4294967296 | bytes 12582912 | tf_op jit(solution)/shard_map/dot_general | solution.py:30
  111.3 89.1 %reduce-scatter.3.cloned.1.call-done = f32[128,1024]{0,1:T(8,128)} async-done(((f32[1024,1024]{0,1:T(8,128)}), f32[128,1024]{0,1:T(8,128)}) %reduce-scatter.3.cloned.1.call-update) | async-done | bytes 524304 | tf_op jit(solution)/shard_map/reduce_scatter | solution.py:36
  201.6 46.4 %all_gather.10 = f32[128,1024]{0,1:T(8,128)} all-gather(f32[128,32]{0,1:T(8,128)S(1)} %slice.242), channel_id=1, replica_groups=mesh['row'=32,'col'=8] {'row'}, dimensions={1}, use_global_device_ids=true | all-gather | bytes 540672 | tf_op jit(solution)/shard_map/all_gather | solution.py:40
  248.4 2.4 fusion.21
  250.9 83.2 %all-gather.5.cloned.1.call-done = f32[1024,1024]{0,1:T(8,128)} async-done(((f32[128,1024]{0,1:T(8,128)}), f32[1024,1024]{0,1:T(8,128)}) %all-gather.5.cloned.1.call-update) | async-done | bytes 4194320 | tf_op jit(solution)/shard_map/all_gather | solution.py:41
  334.0 5.5 copy.3
  339.5 4.4 fusion
  346.0 11.7 %cholesky.223 = f32[128,128]{1,0:T(8,128)S(1)} custom-call(f32[128,128]{1,0:T(8,128)S(1)} %cholesky.580), custom_call_target="Cholesky" | custom-call | tf_op jit(solution)/shard_map/jit(cholesky)/cholesky | solution.py:18
  357.7 9.8 %custom-call.62 = f32[1,128,128]{1,2,0:T(8,128)S(1)} custom-call(f32[1,128,128]{2,1,0:T(8,128)S(1)} %get-tuple-element.69), custom_call_target="InvertDiagBlocksLowerTriangular" | custom-call | tf_op jit(solution)/shard_map/jit(cholesky)/cholesky | solution.py:18
  367.5 2.5 cholesky.255
  373.9 11.9 %cholesky.244 = f32[128,128]{1,0:T(8,128)S(1)} custom-call(f32[128,128]{1,0:T(8,128)S(1)} %cholesky.584), custom_call_target="Cholesky" | custom-call | tf_op jit(solution)/shard_map/jit(cholesky)/cholesky | solution.py:18
  386.5 9.8 %custom-call.63 = f32[1,128,128]{1,2,0:T(8,128)S(1)} custom-call(f32[1,128,128]{2,1,0:T(8,128)S(1)} %get-tuple-element.66), custom_call_target="InvertDiagBlocksLowerTriangular" | custom-call | tf_op jit(solution)/shard_map/jit(cholesky)/cholesky | solution.py:18
  399.6 11.7 %cholesky.468 = f32[128,128]{1,0:T(8,128)S(1)} custom-call(f32[128,128]{1,0:T(8,128)S(1)} %cholesky.589), custom_call_target="Cholesky" | custom-call | tf_op jit(solution)/shard_map/jit(cholesky)/cholesky | solution.py:18
  412.7 9.8 %custom-call.64 = f32[1,128,128]{1,2,0:T(8,128)S(1)} custom-call(f32[1,128,128]{2,1,0:T(8,128)S(1)} %get-tuple-element.63), custom_call_target="InvertDiagBlocksLowerTriangular" | custom-call | tf_op jit(solution)/shard_map/jit(cholesky)/cholesky | solution.py:18
  426.0 12.1 %cholesky.487 = f32[128,128]{1,0:T(8,128)S(1)} custom-call(f32[128,128]{1,0:T(8,128)S(1)} %cholesky.594), custom_call_target="Cholesky" | custom-call | tf_op jit(solution)/shard_map/jit(cholesky)/cholesky | solution.py:18
  439.4 9.8 %custom-call.65 = f32[1,128,128]{1,2,0:T(8,128)S(1)} custom-call(f32[1,128,128]{2,1,0:T(8,128)S(1)} %get-tuple-element.60), custom_call_target="InvertDiagBlocksLowerTriangular" | custom-call | tf_op jit(solution)/shard_map/jit(cholesky)/cholesky | solution.py:18
  452.7 11.7 %cholesky.506 = f32[128,128]{1,0:T(8,128)S(1)} custom-call(f32[128,128]{1,0:T(8,128)S(1)} %cholesky.599), custom_call_target="Cholesky" | custom-call | tf_op jit(solution)/shard_map/jit(cholesky)/cholesky | solution.py:18
  465.8 9.9 %custom-call.66 = f32[1,128,128]{1,2,0:T(8,128)S(1)} custom-call(f32[1,128,128]{2,1,0:T(8,128)S(1)} %get-tuple-element.57), custom_call_target="InvertDiagBlocksLowerTriangular" | custom-call | tf_op jit(solution)/shard_map/jit(cholesky)/cholesky | solution.py:18
  479.1 11.7 %cholesky.526 = f32[128,128]{1,0:T(8,128)S(1)} custom-call(f32[128,128]{1,0:T(8,128)S(1)} %cholesky.604), custom_call_target="Cholesky" | custom-call | tf_op jit(solution)/shard_map/jit(cholesky)/cholesky | solution.py:18
  492.1 9.8 %custom-call.67 = f32[1,128,128]{1,2,0:T(8,128)S(1)} custom-call(f32[1,128,128]{2,1,0:T(8,128)S(1)} %get-tuple-element.54), custom_call_target="InvertDiagBlocksLowerTriangular" | custom-call | tf_op jit(solution)/shard_map/jit(cholesky)/cholesky | solution.py:18
  505.0 11.9 %cholesky.546 = f32[128,128]{1,0:T(8,128)S(1)} custom-call(f32[128,128]{1,0:T(8,128)S(1)} %cholesky.609), custom_call_target="Cholesky" | custom-call | tf_op jit(solution)/shard_map/jit(cholesky)/cholesky | solution.py:18
  518.2 9.8 %custom-call.68 = f32[1,128,128]{1,2,0:T(8,128)S(1)} custom-call(f32[1,128,128]{2,1,0:T(8,128)S(1)} %get-tuple-element.51), custom_call_target="InvertDiagBlocksLowerTriangular" | custom-call | tf_op jit(solution)/shard_map/jit(cholesky)/cholesky | solution.py:18
  530.6 11.7 %cholesky.564 = f32[128,128]{1,0:T(8,128)S(1)} custom-call(f32[128,128]{1,0:T(8,128)S(1)} %convolution_subtract_fusion.11), custom_call_target="Cholesky" | custom-call | tf_op jit(solution)/shard_map/jit(cholesky)/cholesky | solution.py:18
  549.5 4.8 select_select_fusion
  554.3 22.5 %while.1 = (s32[]{:T(128)}, f32[1024,1024]{1,0:T(8,128)}, s32[8,2]{0,1:T(2,128)S(1)}, f32[8,128,128]{2,1,0:T(8,128)S(1)}, s32[]{:T(128)}) while((s32[]{:T(128)}, f32[1024,1024]{1,0:T(8,128)}, s32[8,2]{0,1:T(2,128)S(1)}, f32[8,128,128]{2,1,0:T(8,128)S(1)}, s32[]{:T(128)}) %tuple.57), condition=%wide.while_cond, body=%wide.while_body.sunk | while | flops 2 | bytes 131189 | solution.py:20
  576.8 79.0 %custom-call.69 = f32[8,128,128]{1,2,0:T(8,128)S(1)} custom-call(f32[8,128,128]{2,1,0:T(8,128)S(1)} %get-tuple-element.12), custom_call_target="InvertDiagBlocksLowerTriangular" | custom-call | tf_op jit(solution)/shard_map/triangular_solve | solution.py:20
  667.2 2.6 convolution_subtract_fusion.2
  670.5 2.8 convolution_subtract_fusion.1
  674.0 3.4 convolution_subtract_fusion.3
  678.0 5.0 fusion.30
  683.0 96.7 %reduce-scatter.5.cloned.1.call-done = f32[128,1024]{1,0:T(8,128)} async-done(((f32[1024,1024]{1,0:T(8,128)}), f32[128,1024]{1,0:T(8,128)}) %reduce-scatter.5.cloned.1.call-update) | async-done | bytes 524304 | tf_op jit(solution)/shard_map/reduce_scatter | solution.py:44
  (93 shorter events, 73.4 us)
Async XLA Ops:
  6.5 94.7 %all-gather.3.cloned.1.call-start = ((), (), s32[]{:S(2)}) async-start(), calls=%async_computation.2 | async-start | bytes 4325376 | tf_op jit(solution)/shard_map/all_gather | solution.py:31
  8.1 192.2 %reduce-scatter.3.cloned.1.call-start = ((), (), s32[]{:S(2)}) async-start(), calls=%async_computation.3 | async-start | bytes 4718592 | tf_op jit(solution)/shard_map/reduce_scatter | solution.py:36
  111.2 222.9 %all-gather.5.cloned.1.call-start = ((), (), s32[]{:S(2)}) async-start(), calls=%async_computation.4 | async-start | bytes 4718592 | tf_op jit(solution)/shard_map/all_gather | solution.py:41
  248.0 531.7 %reduce-scatter.5.cloned.1.call-start = ((), (), s32[]{:S(2)}) async-start(), calls=%async_computation.5 | async-start | bytes 4718592 | tf_op jit(solution)/shard_map/reduce_scatter | solution.py:44
  344.0 2.0 copy-start.1
  655.8 3.2 copy-start
Sparse Core Ops, SparseCore 0:
  10.1 91.0 all-gather.2
  111.3 89.0 reduce-scatter.2
  248.2 85.8 all-gather.4
  683.2 96.5 reduce-scatter.4
where the time goes:
time: 792 us; the launch traced here: 787 us
  waiting for transfers between devices  362 us (46%)
  other arithmetic  265 us (33%)
  matrix products  60.1 us (8%)
  blocking collectives  46.4 us (6%)
  local copies, waits for them, and re-layouts  33.9 us (4%)
  between operations  18.8 us (2%)
    another operation x30, other arithmetic, lower_inverse(): factor = jnp.linalg.cholesky(block)  173 us
    reduce_scatter x1, waiting for transfers between devices, shards(): lax.psum_scatter(jnp.dot(own_cols, gram, precision=lax.Precision.HIGHEST)...  96.7 us
    all_gather x1, waiting for transfers between devices, shards(): lax.all_gather(panel_local, 'row', axis=0, tiled=True)  93.1 us
    reduce_scatter x1, waiting for transfers between devices, shards(): lax.psum_scatter(partial_gram, 'col', scatter_dimension=0, tiled=True)  89.1 us
    another operation x3, other arithmetic, lower_inverse(): lax.linalg.triangular_solve(factor, identity, left_side=True, lower=True)  83.8 us
    all_gather x1, waiting for transfers between devices, shards(): diag_block = lax.all_gather(wide_cols, 'col', axis=0, tiled=True)  83.2 us
    all_gather x1, blocking collectives, shards(): wide_cols = lax.all_gather(gram[:, :per_row], 'row', axis=1, tiled=True)  46.4 us
    another operation x14, matrix products, lower_inverse(): factor = jnp.linalg.cholesky(block)  23.1 us
  transfers between devices with their start and end apart: 4, of which 4 were waited for; matrix products, arithmetic and copies ran while one was open for 0% of the time, Pallas kernels for 0%

commit v1 on v0

v1 whole, which is shorter than its diff:
```python
import functools

import jax
import jax.numpy as jnp
from jax import lax
from jax.experimental import pallas as pl
from jax.experimental.pallas import tpu as pltpu
from jax.sharding import PartitionSpec as P

M = 16384
PANEL = 1024
PB = 32
NB = 8
BK = 128
RIDGE = 0.001
MESH = pl.DeviceIdType.MESH
F32 = jnp.float32
BF16 = jnp.bfloat16


def split3(x):
    high = x.astype(BF16)
    rest = x - high.astype(F32)
    mid = rest.astype(BF16)
    low = (rest - mid.astype(F32)).astype(BF16)
    return high, mid, low


def stack_left(x, axis=1):
    high, mid, low = split3(x)
    return jnp.concatenate([high, high, high, mid, mid, low], axis=axis)


def stack_right(x, axis=1):
    high, mid, low = split3(x)
    return jnp.concatenate([high, mid, low, high, mid, high], axis=axis)


def dot_nt(a, b):
    return lax.dot_general(a, b, (((1,), (1,)), ((), ())), preferred_element_type=F32)


def dot_nn(a, b):
    return lax.dot_general(a, b, (((1,), (0,)), ((), ())), preferred_element_type=F32)


def recip(x):
    return pltpu.reciprocal(x, approx=True)


def row_of(x, i):
    return jnp.broadcast_to(x[i : i + 1, :], (8, BK))


def col_of(x, j):
    return jnp.broadcast_to(x[:, j : j + 1], (8, BK))


def factor8(c):
    w = [[None] * 8 for _ in range(8)]
    rp = [None] * 8
    for i in range(8):
        w[i][i] = jnp.ones_like(c[0][0])
    for s in range(8):
        rp[s] = recip(c[s][s])
        for i in range(s + 1, 8):
            f = c[i][s] * rp[s]
            for j in range(s + 1, i + 1):
                c[i][j] = c[i][j] - f * c[j][s]
            for q in range(s):
                w[i][q] = w[i][q] - f * w[s][q]
            w[i][s] = -f
    return w, rp


def factor_inverse(a):
    tiles = [a[8 * t : 8 * t + 8, :] for t in range(16)]
    lane = lax.broadcasted_iota(jnp.int32, (8, BK), 1)
    sub = lax.broadcasted_iota(jnp.int32, (8, BK), 0)
    out = []
    for t in range(16):
        x, b0 = tiles[t], 8 * t
        cols = [col_of(x, b0 + j) for j in range(8)]
        w, rp = factor8([[row_of(cols[j], i) for j in range(i + 1)] for i in range(8)])
        inside = (lane >= b0) & (lane < b0 + 8)
        xt = jnp.where(inside, (lane - b0 == sub).astype(F32), x)
        r = [row_of(xt, i) for i in range(8)]
        u = []
        for s in range(8):
            y = r[s]
            for j in range(s):
                y = y + w[s][j] * r[j]
            u.append(y)
        y, p = u[0], rp[0]
        for s in range(1, 8):
            y = jnp.where(sub == s, u[s], y)
            p = jnp.where(sub == s, rp[s], p)
        out.append(jnp.where(lane <= b0 + sub, y * lax.sqrt(p), 0.0))
        for i in range(t + 1, 16):
            e = [col_of(tiles[i], b0 + j) for j in range(8)]
            z = jnp.where(inside, 0.0, tiles[i])
            for s in range(8):
                f = e[s]
                for j in range(s):
                    f = f + w[s][j] * e[j]
                z = z - (f * rp[s]) * u[s]
            tiles[i] = z
    return jnp.concatenate(out, axis=0)


def cholesky_panels(a_ref, inv_ref, left_ref, right_ref):
    rows = lax.broadcasted_iota(jnp.int32, (PANEL, BK), 0)

    def step(k, carry):
        here = pl.ds(pl.multiple_of(k * BK, BK), BK)
        inverse = factor_inverse(a_ref[here, here])
        inv_ref[k] = inverse
        panel = dot_nt(stack_left(a_ref[:, here]), stack_right(inverse))
        panel = jnp.where(rows >= (k + 1) * BK, panel, 0.0)
        a_ref[:, here] = panel
        left_ref[...] = stack_left(panel)
        right_ref[...] = stack_right(panel)

        def update(j, inner):
            cols = pl.ds(pl.multiple_of(j * 2 * BK, 2 * BK), 2 * BK)
            a_ref[:, cols] -= jnp.where(
                lax.broadcasted_iota(jnp.int32, (PANEL, 2 * BK), 1) + j * 2 * BK >= (k + 1) * BK,
                dot_nt(left_ref[...], right_ref[cols, :]),
                0.0,
            )
            return inner

        lax.fori_loop((k + 1) // 2, NB // 2, update, 0)
        return carry

    lax.fori_loop(0, NB, step, 0)


def kernel(
    markers_ref, out_ref,
    own, panel, a_ref, dpart, drecv, dred, gsend, grecv, solved, inv_ref, left_ref, right_ref,
    local_sem, ag_send, ag_recv, dag_send, dag_recv, rs_send, rs_recv, dc_send, dc_recv,
    gs_send, gs_recv, os_send, os_recv,
):
    row = lax.axis_index("row")
    col = lax.axis_index("col")
    core = lax.rem(row, 2)
    z = lax.rem(row // 2, 8)
    hi = row // 16

    def row_id(h, zz, q):
        return h * 16 + zz * 2 + q

    sibling = row_id(hi, z, 1 - core)
    partner = row_id(1 - hi, z, core)
    up = row_id(hi, lax.rem(z + 1, 8), core)
    down = row_id(hi, lax.rem(z + 7, 8), core)
    row_peers = (sibling, partner, up, down)
    col_peers = [lax.rem(col + o, NB) for o in range(1, NB)]

    load_panel = pltpu.make_async_copy(
        markers_ref.at[pl.ds(0, PB), :], panel.at[pl.ds(pl.multiple_of(row * PB, PB), PB), :], local_sem.at[0]
    )
    load_panel.start()
    load_own = pltpu.make_async_copy(markers_ref, own, local_sem.at[1])
    load_own.start()

    barrier = pltpu.get_barrier_semaphore()
    for peer in row_peers:
        pl.semaphore_signal(barrier, inc=1, device_id=(peer, col), device_id_type=MESH)
    for peer in col_peers:
        pl.semaphore_signal(barrier, inc=1, device_id=(row, peer), device_id_type=MESH)
    pl.semaphore_wait(barrier, len(row_peers) + len(col_peers))

    def gather(buf, send, recv, between):
        def block(r):
            return buf.at[pl.ds(pl.multiple_of(r * PB, PB), PB), :]

        started = []

        def copy(r, target, index, go=True):
            c = pltpu.make_async_remote_copy(
                src_ref=block(r), dst_ref=block(r), send_sem=send.at[index], recv_sem=recv.at[index],
                device_id=(target, col), device_id_type=MESH,
            )
            if go:
                c.start()
                started.append(c)
            return c

        def index_of(stream, way, d):
            return (stream * 2 + way) * 4 + d - 1

        def source(stream, way, d):
            h = hi if stream == 0 else 1 - hi
            zz = lax.rem(z + (8 - d if way == 0 else d), 8)
            return row_id(h, zz, core)

        def forward(stream, way, d):
            copy(source(stream, way, d), up if way == 0 else down, index_of(stream, way, d + 1))

        reach = {(0, 0): 4, (0, 1): 3, (1, 0): 3, (1, 1): 4}
        sib = 16
        own_r = row
        part_r = partner
        copy(own_r, partner, 32)
        forward(0, 0, 0)
        forward(0, 1, 0)
        copy(own_r, sibling, sib + 0)
        between(0)
        copy(part_r, partner, 32, go=False).wait_recv()
        forward(1, 0, 0)
        forward(1, 1, 0)
        copy(part_r, sibling, sib + 1)
        n = 2
        sib_sources = [row_id(hi, z, 1 - core), row_id(1 - hi, z, 1 - core)]
        between(1)
        for d in range(1, 5):
            for stream in (0, 1):
                for way in (0, 1):
                    if d > reach[stream, way]:
                        continue
                    r = source(stream, way, d)
                    copy(r, sibling, index_of(stream, way, d), go=False).wait_recv()
                    if d < reach[stream, way]:
                        forward(stream, way, d)
                    copy(r, sibling, sib + n)
                    sib_sources.append(r + 1 - 2 * core)
                    n += 1
            between(d + 1)
        for i, r in enumerate(sib_sources):
            copy(r, sibling, sib + i, go=False).wait_recv()
        return started

    load_panel.wait()
    started = gather(panel, ag_send, ag_recv, lambda s: None)

    mine = pl.ds(pl.multiple_of(row * PB, PB), PB)
    dpart[...] = dot_nt(panel[mine, :], panel[...])

    def reduce_copy(o, target):
        return pltpu.make_async_remote_copy(
            src_ref=dpart.at[:, pl.ds(pl.multiple_of(target * BK, BK), BK)], dst_ref=drecv.at[o],
            send_sem=rs_send.at[o], recv_sem=rs_recv.at[o], device_id=(row, target), device_id_type=MESH,
        )

    scatter = [reduce_copy(o, col_peers[o - 1]) for o in range(1, NB)]
    for c in scatter:
        c.start()
    load_own.wait()
    parity = lax.rem(col, 2)

    def gram_pair(i):
        pair = lax.rem(col // 2 + i, NB // 2)
        both = dot_nt(panel[...], own[pl.ds(pl.multiple_of(pair * 2 * BK, 2 * BK), 2 * BK), :])
        gsend[2 * i + parity] = both[:, :BK]
        gsend[2 * i + 1 - parity] = both[:, BK:]

    gram_pair(1)
    for c in scatter:
        c.wait_recv()
    here = pl.ds(pl.multiple_of(col * BK, BK), BK)
    total = dpart[:, here]
    for o in range(1, NB):
        total = total + drecv[o]
    diagonal = (
        lax.broadcasted_iota(jnp.int32, (PB, BK), 0) + row * PB
        == lax.broadcasted_iota(jnp.int32, (PB, BK), 1) + col * BK
    )
    dred[...] = total * (1.0 / M) + jnp.where(diagonal, RIDGE, 0.0)
    a_ref[mine, here] = dred[...]

    def spread_copy(o, target):
        return pltpu.make_async_remote_copy(
            src_ref=dred, dst_ref=a_ref.at[mine, here],
            send_sem=dc_send.at[o], recv_sem=dc_recv.at[o], device_id=(row, target), device_id_type=MESH,
        )

    spread = [spread_copy(o, col_peers[o - 1]) for o in range(1, NB)]
    for c in spread:
        c.start()
    gram_pair(2)
    for c in spread:
        c.wait_recv()

    gram_copies = []

    def gram_copy(i, same):
        target = 2 * lax.rem(col // 2 + i, NB // 2) + (parity if same else 1 - parity)
        slot = 2 * i + (0 if same else 1)
        c = pltpu.make_async_remote_copy(
            src_ref=gsend.at[slot], dst_ref=grecv.at[slot],
            send_sem=gs_send.at[slot], recv_sem=gs_recv.at[slot], device_id=(row, target), device_id_type=MESH,
        )
        c.start()
        gram_copies.append(c)

    def between(s):
        if s == 0:
            gram_pair(3)
        elif s == 1:
            for i in (1, 2, 3):
                gram_copy(i, True)
                gram_copy(i, False)
            gram_pair(0)
            gram_copy(0, False)

    started += gather(a_ref, dag_send, dag_recv, between)

    for c in started + scatter + spread:
        c.wait_send()
    cholesky_panels(a_ref, inv_ref, left_ref, right_ref)

    for c in gram_copies:
        c.wait()
    total = gsend[0]
    for s in range(1, NB):
        total = total + grecv[s]
    ridge = (
        (lax.broadcasted_iota(jnp.int32, (PANEL, BK), 0) == lax.broadcasted_iota(jnp.int32, (PANEL, BK), 1) + row * PB)
        & (lax.broadcasted_iota(jnp.int32, (PANEL, BK), 1) < PB)
        & (col == 0)
    )
    solved[...] = total * (1.0 / M) + jnp.where(ridge, RIDGE, 0.0)

    def out_copy(k, source):
        return pltpu.make_async_remote_copy(
            src_ref=solved.at[pl.ds(k * BK, BK), :], dst_ref=out_ref.at[:, pl.ds(pl.multiple_of(source * BK, BK), BK)],
            send_sem=os_send.at[k], recv_sem=os_recv.at[source], device_id=(row, k), device_id_type=MESH,
        )

    for k in range(NB):
        s_k = dot_nn(stack_left(inv_ref[k]), stack_right(solved[k * BK : (k + 1) * BK, :], axis=0))
        solved[k * BK : (k + 1) * BK, :] = s_k

        @pl.when(col != k)
        def _():
            out_copy(k, col).start()

        @pl.when(col == k)
        def _():
            out_ref[:, here] = s_k

        if k < NB - 1:
            rest = slice((k + 1) * BK, PANEL)
            solved[rest, :] -= dot_nn(
                stack_left(a_ref[rest, k * BK : (k + 1) * BK]), stack_right(s_k, axis=0)
            )
    for k in range(NB):
        @pl.when(col != k)
        def _():
            out_copy(k, col).wait_send()
            out_copy(k, jnp.int32(k)).wait_recv()


def shards(markers):
    sem = pltpu.SemaphoreType.DMA
    return pl.pallas_call(
        kernel,
        out_shape=jax.ShapeDtypeStruct((BK, 1024), F32),
        in_specs=[pl.BlockSpec(memory_space=pl.ANY)],
        out_specs=pl.BlockSpec(memory_space=pltpu.VMEM),
        scratch_shapes=[
            pltpu.VMEM((1024, 2048), BF16),
            pltpu.VMEM((PANEL, 2048), BF16),
            pltpu.VMEM((PANEL, PANEL), F32),
            pltpu.VMEM((PB, PANEL), F32),
            pltpu.VMEM((NB, PB, BK), F32),
            pltpu.VMEM((PB, BK), F32),
            pltpu.VMEM((NB, PANEL, BK), F32),
            pltpu.VMEM((NB, PANEL, BK), F32),
            pltpu.VMEM((PANEL, BK), F32),
            pltpu.VMEM((NB, BK, BK), F32),
            pltpu.VMEM((PANEL, 6 * BK), BF16),
            pltpu.VMEM((PANEL, 6 * BK), BF16),
            sem((2,)), sem((33,)), sem((33,)), sem((33,)), sem((33,)),
            sem((NB,)), sem((NB,)), sem((NB,)), sem((NB,)),
            sem((NB,)), sem((NB,)), sem((NB,)), sem((NB,)),
        ],
        compiler_params=pltpu.CompilerParams(
            collective_id=0, has_side_effects=True, vmem_limit_bytes=58 * 1024 * 1024
        ),
    )(markers)


def solution(mesh):
    return jax.shard_map(
        shards, mesh=mesh, in_specs=(P("row", "col"),), out_specs=P("col", "row"), check_vma=False
    )
```

time: 792 us -> 141 us (0.18)
  waiting for transfers between devices: 362 us -> 0 us
  other arithmetic: 265 us -> 0 us
  Pallas kernels: 0 us -> 139 us
  matrix products: 60.1 us -> 0 us
  blocking collectives: 46.4 us -> 0 us
  local copies, waits for them, and re-layouts: 33.9 us -> 1.89 us
  between operations: 18.8 us -> 0.01 us
    another operation x33 -> x0, other arithmetic: 256 us -> none  [the longest x30 173 us: lower_inverse(): factor = jnp.linalg.cholesky(block)]
    reduce_scatter x2 -> x0, waiting for transfers between devices: 186 us -> none  [the longest x1 96.7 us: shards(): lax.psum_scatter(jnp.dot(own_cols, gram, precision=lax.Precision.HIGHEST)...]
    all_gather x2 -> x0, waiting for transfers between devices: 176 us -> none  [the longest x1 93.1 us: shards(): lax.all_gather(panel_local, 'row', axis=0, tiled=True)]
    pallas_call x0 -> x1, Pallas kernels: none -> 139 us  [shards(): pl.pallas_call(kernel, out_shape=jax.ShapeDtypeStruct((BK, 1024), F32), i...]
    all_gather x1 -> x0, blocking collectives: 46.4 us -> none  [shards(): wide_cols = lax.all_gather(gram[:, :per_row], 'row', axis=1, tiled=True)]
    another operation x29 -> x0, matrix products: 45.2 us -> none  [the longest x14 23.1 us: lower_inverse(): factor = jnp.linalg.cholesky(block)]
    another operation x33 -> x0, local copies, waits for them, and re-layouts: 24.9 us -> none
    dot_general x2 -> x0, matrix products: 14.9 us -> none  [the longest x1 9.91 us: shards(): lax.dot_general(lax.all_gather(panel_local, 'row', axis=0, tiled=True), m...]
  transfers between devices with their start and end apart: 4 -> 0, of which waited for: 4 -> 0; matrix products, arithmetic and copies ran while one was open for 0% -> 0% of each run, Pallas kernels for 0% -> 0%
where the time goes in v1:
time: 141 us
  Pallas kernels  139 us (99%)
  local copies, waits for them, and re-layouts  1.89 us (1%)
    pallas_call x1, Pallas kernels, shards(): pl.pallas_call(kernel, out_shape=jax.ShapeDtypeStruct((BK, 1024), F32), i...  139 us

profile of v1, /device:TPU:1, one launch (start us, length us, event | category | flops | bytes accessed | tf_op | source)
XLA Modules:
  0.0 141.1 jit_solution(12095885332757896770)
XLA Ops:
  0.0 139.2 %shard_map.17 = f32[128,1024]{1,0:T(8,128)} custom-call(bf16[1024,2048]{1,0:T(8,128)(2,1)} %markers_ref.1), custom_call_target="tpu_custom_call" | custom-call | tf_op jit(solution)/shard_map/pallas_call | solution.py:358
  139.2 1.9 %copy.3 = f32[128,1024]{1,0:T(8,128)} copy(f32[128,1024]{1,0:T(8,128)} %shard_map.17) | data formatting | bytes 1048576

commit v2 on v1

--- a/solution.py
+++ b/solution.py
@@ -108,37 +108,47 @@
     return jnp.concatenate(out, axis=0)
 
 
-def cholesky_panels(a_ref, inv_ref, left_ref, right_ref):
+def block_at(k):
+    return pl.ds(pl.multiple_of(k * BK, BK), BK)
+
+
+def factor_steps(a_ref, g_ref, diag, left_ref, right_ref, invl_ref, invr_ref, emit):
     rows = lax.broadcasted_iota(jnp.int32, (PANEL, BK), 0)
+    diag[...] = a_ref[:BK, :BK]
+    invl_ref[...] = jnp.zeros_like(invl_ref)
+    invr_ref[...] = jnp.zeros_like(invr_ref)
 
     def step(k, carry):
-        here = pl.ds(pl.multiple_of(k * BK, BK), BK)
-        inverse = factor_inverse(a_ref[here, here])
-        inv_ref[k] = inverse
-        panel = dot_nt(stack_left(a_ref[:, here]), stack_right(inverse))
-        panel = jnp.where(rows >= (k + 1) * BK, panel, 0.0)
-        a_ref[:, here] = panel
+        here = block_at(k)
+        before = block_at(jnp.maximum(k - 1, 0))
+        after = block_at(jnp.minimum(k + 1, NB - 1))
+        block = diag[...]
+        s_k = dot_nn(invl_ref[...], stack_right(g_ref[before, :], axis=0))
+        panel = dot_nt(stack_left(a_ref[:, before]), invr_ref[...])
+        panel = jnp.where(rows >= k * BK, panel, 0.0)
         left_ref[...] = stack_left(panel)
         right_ref[...] = stack_right(panel)
-
-        def update(j, inner):
-            cols = pl.ds(pl.multiple_of(j * 2 * BK, 2 * BK), 2 * BK)
-            a_ref[:, cols] -= jnp.where(
-                lax.broadcasted_iota(jnp.int32, (PANEL, 2 * BK), 1) + j * 2 * BK >= (k + 1) * BK,
-                dot_nt(left_ref[...], right_ref[cols, :]),
-                0.0,
-            )
-            return inner
-
-        lax.fori_loop((k + 1) // 2, NB // 2, update, 0)
+        for j in range(NB // 2):
+            cols = slice(2 * BK * j, 2 * BK * (j + 1))
+            a_ref[:, cols] -= dot_nt(left_ref[...], right_ref[cols, :])
+        g_ref[...] -= dot_nn(left_ref[...], stack_right(s_k, axis=0))
+        inverse = factor_inverse(block)
+        inv_r = stack_right(inverse)
+        invl_ref[...] = stack_left(inverse)
+        invr_ref[...] = inv_r
+        low = dot_nt(stack_left(a_ref[after, here]), inv_r)
+        diag[...] = a_ref[after, after] - dot_nt(stack_left(low), stack_right(low))
+        emit(k - 1, s_k)
         return carry
 
     lax.fori_loop(0, NB, step, 0)
+    last = slice(PANEL - BK, PANEL)
+    emit(NB - 1, dot_nn(invl_ref[...], stack_right(g_ref[last, :], axis=0)))
 
 
 def kernel(
     markers_ref, out_ref,
-    own, panel, a_ref, dpart, drecv, dred, gsend, grecv, solved, inv_ref, left_ref, right_ref,
+    own, panel, a_ref, dpart, drecv, dred, gsend, grecv, g_ref, solved, diag, left_ref, right_ref, invl_ref, invr_ref,
     local_sem, ag_send, ag_recv, dag_send, dag_recv, rs_send, rs_recv, dc_send, dc_recv,
     gs_send, gs_recv, os_send, os_recv,
 ):
@@ -171,6 +181,9 @@
     for peer in col_peers:
         pl.semaphore_signal(barrier, inc=1, device_id=(row, peer), device_id_type=MESH)
     pl.semaphore_wait(barrier, len(row_peers) + len(col_peers))
+
+    def piece_id(h, zz):
+        return h * 8 + zz
 
     def gather(buf, send, recv, between):
         def block(r):
@@ -201,41 +214,85 @@
 
         reach = {(0, 0): 4, (0, 1): 3, (1, 0): 3, (1, 1): 4}
         sib = 16
-        own_r = row
-        part_r = partner
-        copy(own_r, partner, 32)
+        sib_done = []
+
+        def to_sibling(r, index):
+            copy(r, sibling, index)
+            sib_done.append(copy(r + 1 - 2 * core, sibling, index, go=False))
+
+        def from_sibling():
+            for c in sib_done:
+                c.wait_recv()
+            sib_done.clear()
+
+        copy(row, partner, 32)
         forward(0, 0, 0)
         forward(0, 1, 0)
-        copy(own_r, sibling, sib + 0)
-        between(0)
-        copy(part_r, partner, 32, go=False).wait_recv()
+        to_sibling(row, sib)
+        copy(partner, partner, 32, go=False).wait_recv()
         forward(1, 0, 0)
         forward(1, 1, 0)
-        copy(part_r, sibling, sib + 1)
+        to_sibling(partner, sib + 1)
         n = 2
-        sib_sources = [row_id(hi, z, 1 - core), row_id(1 - hi, z, 1 - core)]
-        between(1)
         for d in range(1, 5):
-            for stream in (0, 1):
-                for way in (0, 1):
-                    if d > reach[stream, way]:
-                        continue
-                    r = source(stream, way, d)
-                    copy(r, sibling, index_of(stream, way, d), go=False).wait_recv()
-                    if d < reach[stream, way]:
-                        forward(stream, way, d)
-                    copy(r, sibling, sib + n)
-                    sib_sources.append(r + 1 - 2 * core)
-                    n += 1
-            between(d + 1)
-        for i, r in enumerate(sib_sources):
-            copy(r, sibling, sib + i, go=False).wait_recv()
+            ways = [sw for sw in ((0, 0), (0, 1), (1, 0), (1, 1)) if d <= reach[sw]]
+            arrived = []
+            for stream, way in ways:
+                r = source(stream, way, d)
+                copy(r, sibling, index_of(stream, way, d), go=False).wait_recv()
+                if d < reach[stream, way]:
+                    forward(stream, way, d)
+                arrived.append(r)
+            from_sibling()
+            for r in arrived:
+                to_sibling(r, sib + n)
+                n += 1
+            between(d)
+        from_sibling()
         return started
 
+    def pieces(d):
+        if d == 0:
+            return [piece_id(hi, z), piece_id(1 - hi, z)]
+        plus, minus = lax.rem(z + 8 - d, 8), lax.rem(z + d, 8)
+        if d == 4:
+            return [piece_id(hi, plus), piece_id(1 - hi, plus)]
+        return [piece_id(hi, plus), piece_id(hi, minus), piece_id(1 - hi, plus), piece_id(1 - hi, minus)]
+
+    first_tile = [0, 1, 3, 5, 7]
+    gram_copies = []
+
+    def gram_chunk(d):
+        ids = pieces(d)
+        tiles = len(ids) // 2
+        t0 = first_tile[d]
+        chosen = jnp.concatenate([panel[pl.ds(pl.multiple_of(p * 64, 64), 64), :] for p in ids], axis=0)
+        sums = dot_nt(own[...], chosen)
+        for dest in range(NB):
+            slot = lax.rem(dest + NB - col, NB)
+            for t in range(tiles):
+                gsend[t0 + t, slot] = sums[dest * BK : (dest + 1) * BK, t * BK : (t + 1) * BK]
+        for o in range(1, NB):
+            c = pltpu.make_async_remote_copy(
+                src_ref=gsend.at[pl.ds(t0, tiles), o], dst_ref=grecv.at[pl.ds(t0, tiles), o],
+                send_sem=gs_send.at[d * NB + o], recv_sem=gs_recv.at[d * NB + o],
+                device_id=(row, col_peers[o - 1]), device_id_type=MESH,
+            )
+            c.start()
+            gram_copies.append(c)
+
     load_panel.wait()
-    started = gather(panel, ag_send, ag_recv, lambda s: None)
+
+    def while_gathering(d):
+        if d == 1:
+            load_own.wait()
+        if d < 4:
+            gram_chunk(d - 1)
+
+    started = gather(panel, ag_send, ag_recv, while_gathering)
 
     mine = pl.ds(pl.multiple_of(row * PB, PB), PB)
+    here = pl.ds(pl.multiple_of(col * BK, BK), BK)
     dpart[...] = dot_nt(panel[mine, :], panel[...])
 
     def reduce_copy(o, target):
@@ -247,19 +304,9 @@
     scatter = [reduce_copy(o, col_peers[o - 1]) for o in range(1, NB)]
     for c in scatter:
         c.start()
-    load_own.wait()
-    parity = lax.rem(col, 2)
-
-    def gram_pair(i):
-        pair = lax.rem(col // 2 + i, NB // 2)
-        both = dot_nt(panel[...], own[pl.ds(pl.multiple_of(pair * 2 * BK, 2 * BK), 2 * BK), :])
-        gsend[2 * i + parity] = both[:, :BK]
-        gsend[2 * i + 1 - parity] = both[:, BK:]
-
-    gram_pair(1)
+    gram_chunk(3)
     for c in scatter:
         c.wait_recv()
-    here = pl.ds(pl.multiple_of(col * BK, BK), BK)
     total = dpart[:, here]
     for o in range(1, NB):
         total = total + drecv[o]
@@ -279,78 +326,54 @@
     spread = [spread_copy(o, col_peers[o - 1]) for o in range(1, NB)]
     for c in spread:
         c.start()
-    gram_pair(2)
+    gram_chunk(4)
     for c in spread:
         c.wait_recv()
 
-    gram_copies = []
-
-    def gram_copy(i, same):
-        target = 2 * lax.rem(col // 2 + i, NB // 2) + (parity if same else 1 - parity)
-        slot = 2 * i + (0 if same else 1)
-        c = pltpu.make_async_remote_copy(
-            src_ref=gsend.at[slot], dst_ref=grecv.at[slot],
-            send_sem=gs_send.at[slot], recv_sem=gs_recv.at[slot], device_id=(row, target), device_id_type=MESH,
-        )
-        c.start()
-        gram_copies.append(c)
-
-    def between(s):
-        if s == 0:
-            gram_pair(3)
-        elif s == 1:
-            for i in (1, 2, 3):
-                gram_copy(i, True)
-                gram_copy(i, False)
-            gram_pair(0)
-            gram_copy(0, False)
-
-    started += gather(a_ref, dag_send, dag_recv, between)
-
-    for c in started + scatter + spread:
-        c.wait_send()
-    cholesky_panels(a_ref, inv_ref, left_ref, right_ref)
+    def while_spreading(d):
+        pass
+
+    started += gather(a_ref, dag_send, dag_recv, while_spreading)
 
     for c in gram_copies:
-        c.wait()
-    total = gsend[0]
-    for s in range(1, NB):
-        total = total + grecv[s]
+        c.wait_recv()
+    for d in range(5):
+        ids = pieces(d)
+        for t in range(len(ids) // 2):
+            tile = first_tile[d] + t
+            total = gsend[tile, 0]
+            for s in range(1, NB):
+                total = total + grecv[tile, s]
+            total = jnp.transpose(total) * (1.0 / M)
+            for half in range(2):
+                g_ref[pl.ds(pl.multiple_of(ids[2 * t + half] * 64, 64), 64), :] = total[half * 64 : half * 64 + 64, :]
     ridge = (
-        (lax.broadcasted_iota(jnp.int32, (PANEL, BK), 0) == lax.broadcasted_iota(jnp.int32, (PANEL, BK), 1) + row * PB)
-        & (lax.broadcasted_iota(jnp.int32, (PANEL, BK), 1) < PB)
+        (lax.broadcasted_iota(jnp.int32, (PB, BK), 0) == lax.broadcasted_iota(jnp.int32, (PB, BK), 1))
         & (col == 0)
     )
-    solved[...] = total * (1.0 / M) + jnp.where(ridge, RIDGE, 0.0)
+    g_ref[mine, :] += jnp.where(ridge, RIDGE, 0.0)
+    for c in started + scatter + spread + gram_copies:
+        c.wait_send()
 
     def out_copy(k, source):
         return pltpu.make_async_remote_copy(
-            src_ref=solved.at[pl.ds(k * BK, BK), :], dst_ref=out_ref.at[:, pl.ds(pl.multiple_of(source * BK, BK), BK)],
+            src_ref=solved.at[block_at(k), :], dst_ref=out_ref.at[:, pl.ds(pl.multiple_of(source * BK, BK), BK)],
             send_sem=os_send.at[k], recv_sem=os_recv.at[source], device_id=(row, k), device_id_type=MESH,
         )
 
-    for k in range(NB):
-        s_k = dot_nn(stack_left(inv_ref[k]), stack_right(solved[k * BK : (k + 1) * BK, :], axis=0))
-        solved[k * BK : (k + 1) * BK, :] = s_k
-
-        @pl.when(col != k)
+    def emit(k, rows):
+        solved[block_at(jnp.maximum(k, 0)), :] = rows
+
+        @pl.when((k >= 0) & (col != k))
         def _():
             out_copy(k, col).start()
 
-        @pl.when(col == k)
-        def _():
-            out_ref[:, here] = s_k
-
-        if k < NB - 1:
-            rest = slice((k + 1) * BK, PANEL)
-            solved[rest, :] -= dot_nn(
-                stack_left(a_ref[rest, k * BK : (k + 1) * BK]), stack_right(s_k, axis=0)
-            )
-    for k in range(NB):
-        @pl.when(col != k)
-        def _():
-            out_copy(k, col).wait_send()
-            out_copy(k, jnp.int32(k)).wait_recv()
+    factor_steps(a_ref, g_ref, diag, left_ref, right_ref, invl_ref, invr_ref, emit)
+    out_ref[:, here] = solved[here, :]
+    for o in range(1, NB):
+        k = col_peers[o - 1]
+        out_copy(k, col).wait_send()
+        out_copy(k, k).wait_recv()
 
 
 def shards(markers):
@@ -367,15 +390,18 @@
             pltpu.VMEM((PB, PANEL), F32),
             pltpu.VMEM((NB, PB, BK), F32),
             pltpu.VMEM((PB, BK), F32),
-            pltpu.VMEM((NB, PANEL, BK), F32),
-            pltpu.VMEM((NB, PANEL, BK), F32),
+            pltpu.VMEM((NB, NB, BK, BK), F32),
+            pltpu.VMEM((NB, NB, BK, BK), F32),
             pltpu.VMEM((PANEL, BK), F32),
-            pltpu.VMEM((NB, BK, BK), F32),
+            pltpu.VMEM((PANEL, BK), F32),
+            pltpu.VMEM((BK, BK), F32),
             pltpu.VMEM((PANEL, 6 * BK), BF16),
             pltpu.VMEM((PANEL, 6 * BK), BF16),
+            pltpu.VMEM((BK, 6 * BK), BF16),
+            pltpu.VMEM((BK, 6 * BK), BF16),
             sem((2,)), sem((33,)), sem((33,)), sem((33,)), sem((33,)),
             sem((NB,)), sem((NB,)), sem((NB,)), sem((NB,)),
-            sem((NB,)), sem((NB,)), sem((NB,)), sem((NB,)),
+            sem((5 * NB,)), sem((5 * NB,)), sem((NB,)), sem((NB,)),
         ],
         compiler_params=pltpu.CompilerParams(
             collective_id=0, has_side_effects=True, vmem_limit_bytes=58 * 1024 * 1024

time: 141 us -> 153 us (1.085)
  Pallas kernels: 139 us -> 151 us
    pallas_call x1, Pallas kernels: 139 us -> 151 us  [shards(): pl.pallas_call(kernel, out_shape=jax.ShapeDtypeStruct((BK, 1024), F32), i...]
where the time goes in v2:
time: 153 us
  Pallas kernels  151 us (99%)
  local copies, waits for them, and re-layouts  1.89 us (1%)
    pallas_call x1, Pallas kernels, shards(): pl.pallas_call(kernel, out_shape=jax.ShapeDtypeStruct((BK, 1024), F32), i...  151 us

profile of v2, /device:TPU:1, one launch (start us, length us, event | category | flops | bytes accessed | tf_op | source)
XLA Modules:
  0.0 152.6 jit_solution(16954477794032016555)
XLA Ops:
  0.0 150.7 %shard_map.17 = f32[128,1024]{1,0:T(8,128)} custom-call(bf16[1024,2048]{1,0:T(8,128)(2,1)} %markers_ref.1), custom_call_target="tpu_custom_call" | custom-call | tf_op jit(solution)/shard_map/pallas_call | solution.py:381
  150.7 1.9 %copy.3 = f32[128,1024]{1,0:T(8,128)} copy(f32[128,1024]{1,0:T(8,128)} %shard_map.17) | data formatting | bytes 1048576

commit v3 on v2

--- a/solution.py
+++ b/solution.py
@@ -13,6 +13,8 @@
 NB = 8
 BK = 128
 RIDGE = 0.001
+PARTS = 1
+KEPT = 5
 MESH = pl.DeviceIdType.MESH
 F32 = jnp.float32
 BF16 = jnp.bfloat16
@@ -112,7 +114,7 @@
     return pl.ds(pl.multiple_of(k * BK, BK), BK)
 
 
-def factor_steps(a_ref, g_ref, diag, left_ref, right_ref, invl_ref, invr_ref, emit):
+def factor_steps(a_ref, g_ref, diag, left_ref, right_ref, invl_ref, invr_ref, at_first, emit):
     rows = lax.broadcasted_iota(jnp.int32, (PANEL, BK), 0)
     diag[...] = a_ref[:BK, :BK]
     invl_ref[...] = jnp.zeros_like(invl_ref)
@@ -123,6 +125,11 @@
         before = block_at(jnp.maximum(k - 1, 0))
         after = block_at(jnp.minimum(k + 1, NB - 1))
         block = diag[...]
+
+        @pl.when(k == 1)
+        def _():
+            at_first()
+
         s_k = dot_nn(invl_ref[...], stack_right(g_ref[before, :], axis=0))
         panel = dot_nt(stack_left(a_ref[:, before]), invr_ref[...])
         panel = jnp.where(rows >= k * BK, panel, 0.0)
@@ -148,7 +155,7 @@
 
 def kernel(
     markers_ref, out_ref,
-    own, panel, a_ref, dpart, drecv, dred, gsend, grecv, g_ref, solved, diag, left_ref, right_ref, invl_ref, invr_ref,
+    own, panel, a_ref, turned, dpart, drecv, dred, gsend, grecv, relay, g_ref, solved, diag, left_ref, right_ref, invl_ref, invr_ref,
     local_sem, ag_send, ag_recv, dag_send, dag_recv, rs_send, rs_recv, dc_send, dc_recv,
     gs_send, gs_recv, os_send, os_recv,
 ):
@@ -185,15 +192,19 @@
     def piece_id(h, zz):
         return h * 8 + zz
 
-    def gather(buf, send, recv, between):
-        def block(r):
-            return buf.at[pl.ds(pl.multiple_of(r * PB, PB), PB), :]
+    def gather(buf, width, send, recv, between):
+        size = PB // PARTS
+
+        def rows_of(r, part):
+            if part is None:
+                return buf.at[pl.ds(pl.multiple_of(r * PB, PB), PB), pl.ds(0, width)]
+            return buf.at[pl.ds(pl.multiple_of(r * PB + part * size, size), size), pl.ds(0, width)]
 
         started = []
 
-        def copy(r, target, index, go=True):
+        def copy(r, part, target, index, go=True):
             c = pltpu.make_async_remote_copy(
-                src_ref=block(r), dst_ref=block(r), send_sem=send.at[index], recv_sem=recv.at[index],
+                src_ref=rows_of(r, part), dst_ref=rows_of(r, part), send_sem=send.at[index], recv_sem=recv.at[index],
                 device_id=(target, col), device_id_type=MESH,
             )
             if go:
@@ -201,51 +212,50 @@
                 started.append(c)
             return c
 
-        def index_of(stream, way, d):
-            return (stream * 2 + way) * 4 + d - 1
+        def index_of(stream, way, d, part):
+            return 16 + PARTS + ((stream * 2 + way) * 4 + d - 1) * PARTS + part
 
         def source(stream, way, d):
             h = hi if stream == 0 else 1 - hi
             zz = lax.rem(z + (8 - d if way == 0 else d), 8)
             return row_id(h, zz, core)
 
-        def forward(stream, way, d):
-            copy(source(stream, way, d), up if way == 0 else down, index_of(stream, way, d + 1))
+        def forward(stream, way, d, part):
+            copy(source(stream, way, d), part, up if way == 0 else down, index_of(stream, way, d + 1, part))
 
         reach = {(0, 0): 4, (0, 1): 3, (1, 0): 3, (1, 1): 4}
-        sib = 16
         sib_done = []
 
         def to_sibling(r, index):
-            copy(r, sibling, index)
-            sib_done.append(copy(r + 1 - 2 * core, sibling, index, go=False))
+            copy(r, None, sibling, index)
+            sib_done.append(copy(r + 1 - 2 * core, None, sibling, index, go=False))
 
         def from_sibling():
             for c in sib_done:
                 c.wait_recv()
             sib_done.clear()
 
-        copy(row, partner, 32)
-        forward(0, 0, 0)
-        forward(0, 1, 0)
-        to_sibling(row, sib)
-        copy(partner, partner, 32, go=False).wait_recv()
-        forward(1, 0, 0)
-        forward(1, 1, 0)
-        to_sibling(partner, sib + 1)
+        for part in range(PARTS):
+            copy(row, part, partner, 16 + part)
+            forward(0, 0, 0, part)
+            forward(0, 1, 0, part)
+        to_sibling(row, 0)
+        for part in range(PARTS):
+            copy(partner, part, partner, 16 + part, go=False).wait_recv()
+            forward(1, 0, 0, part)
+            forward(1, 1, 0, part)
+        to_sibling(partner, 1)
         n = 2
         for d in range(1, 5):
             ways = [sw for sw in ((0, 0), (0, 1), (1, 0), (1, 1)) if d <= reach[sw]]
-            arrived = []
+            for part in range(PARTS):
+                for stream, way in ways:
+                    copy(source(stream, way, d), part, sibling, index_of(stream, way, d, part), go=False).wait_recv()
+                    if d < reach[stream, way]:
+                        forward(stream, way, d, part)
+            from_sibling()
             for stream, way in ways:
-                r = source(stream, way, d)
-                copy(r, sibling, index_of(stream, way, d), go=False).wait_recv()
-                if d < reach[stream, way]:
-                    forward(stream, way, d)
-                arrived.append(r)
-            from_sibling()
-            for r in arrived:
-                to_sibling(r, sib + n)
+                to_sibling(source(stream, way, d), n)
                 n += 1
             between(d)
         from_sibling()
@@ -262,25 +272,56 @@
     first_tile = [0, 1, 3, 5, 7]
     gram_copies = []
 
+    def col_at(dx, dy):
+        return lax.rem(col // 2 + dx, 4) * 2 + lax.rem(col + dy, 2)
+
+    direct = [(0, 1), (1, 1), (3, 0), (1, 0), (3, 1)]
+
+    def sums_copy(d, slot, target, buf, index, sem):
+        t0, tiles = first_tile[d], len(pieces(d)) // 2
+        c = pltpu.make_async_remote_copy(
+            src_ref=gsend.at[pl.ds(t0, tiles), slot], dst_ref=buf.at[pl.ds(t0, tiles), index],
+            send_sem=gs_send.at[d * NB + sem], recv_sem=gs_recv.at[d * NB + sem],
+            device_id=(row, target), device_id_type=MESH,
+        )
+        c.start()
+        return c
+
+    def direct_copy(d, index):
+        dx, dy = direct[index]
+        gram_copies.append(sums_copy(d, dx * 2 + dy, col_at(dx, dy), grecv, index, index))
+
+    relays = {}
+
     def gram_chunk(d):
         ids = pieces(d)
-        tiles = len(ids) // 2
         t0 = first_tile[d]
         chosen = jnp.concatenate([panel[pl.ds(pl.multiple_of(p * 64, 64), 64), :] for p in ids], axis=0)
         sums = dot_nt(own[...], chosen)
         for dest in range(NB):
-            slot = lax.rem(dest + NB - col, NB)
-            for t in range(tiles):
+            slot = lax.rem(dest // 2 + 4 - col // 2, 4) * 2 + lax.rem(dest % 2 + 2 - lax.rem(col, 2), 2)
+            for t in range(len(ids) // 2):
                 gsend[t0 + t, slot] = sums[dest * BK : (dest + 1) * BK, t * BK : (t + 1) * BK]
-        for o in range(1, NB):
-            c = pltpu.make_async_remote_copy(
-                src_ref=gsend.at[pl.ds(t0, tiles), o], dst_ref=grecv.at[pl.ds(t0, tiles), o],
-                send_sem=gs_send.at[d * NB + o], recv_sem=gs_recv.at[d * NB + o],
-                device_id=(row, col_peers[o - 1]), device_id_type=MESH,
-            )
-            c.start()
-            gram_copies.append(c)
-
+
+    def gram_send(d):
+        relays[d] = [
+            sums_copy(d, 4, col_at(1, 0), relay, 0, 5),
+            sums_copy(d, 5, col_at(3, 0), relay, 1, 6),
+        ]
+        for index in range(3):
+            direct_copy(d, index)
+
+    def gram_relay(d):
+        for c in relays[d]:
+            c.wait_recv()
+        for t in range(first_tile[d], first_tile[d] + len(pieces(d)) // 2):
+            gsend[t, 2] += relay[t, 0]
+            gsend[t, 7] += relay[t, 1]
+        for index in (3, 4):
+            direct_copy(d, index)
+
+    a_ref[...] = jnp.zeros_like(a_ref)
+    g_ref[...] = jnp.zeros_like(g_ref)
     load_panel.wait()
 
     def while_gathering(d):
@@ -288,8 +329,11 @@
             load_own.wait()
         if d < 4:
             gram_chunk(d - 1)
-
-    started = gather(panel, ag_send, ag_recv, while_gathering)
+            gram_send(d - 1)
+        if d > 1:
+            gram_relay(d - 2)
+
+    started = gather(panel, 2048, ag_send, ag_recv, while_gathering)
 
     mine = pl.ds(pl.multiple_of(row * PB, PB), PB)
     here = pl.ds(pl.multiple_of(col * BK, BK), BK)
@@ -315,11 +359,12 @@
         == lax.broadcasted_iota(jnp.int32, (PB, BK), 1) + col * BK
     )
     dred[...] = total * (1.0 / M) + jnp.where(diagonal, RIDGE, 0.0)
-    a_ref[mine, here] = dred[...]
+    kept = block_at(lax.rem(col + NB + KEPT - 1 - row // 4, NB))
+    turned[mine, kept] = dred[...]
 
     def spread_copy(o, target):
         return pltpu.make_async_remote_copy(
-            src_ref=dred, dst_ref=a_ref.at[mine, here],
+            src_ref=dred, dst_ref=turned.at[mine, kept],
             send_sem=dc_send.at[o], recv_sem=dc_recv.at[o], device_id=(row, target), device_id_type=MESH,
         )
 
@@ -331,29 +376,44 @@
         c.wait_recv()
 
     def while_spreading(d):
-        pass
-
-    started += gather(a_ref, dag_send, dag_recv, while_spreading)
-
-    for c in gram_copies:
-        c.wait_recv()
-    for d in range(5):
-        ids = pieces(d)
-        for t in range(len(ids) // 2):
-            tile = first_tile[d] + t
-            total = gsend[tile, 0]
-            for s in range(1, NB):
-                total = total + grecv[tile, s]
-            total = jnp.transpose(total) * (1.0 / M)
-            for half in range(2):
-                g_ref[pl.ds(pl.multiple_of(ids[2 * t + half] * 64, 64), 64), :] = total[half * 64 : half * 64 + 64, :]
-    ridge = (
-        (lax.broadcasted_iota(jnp.int32, (PB, BK), 0) == lax.broadcasted_iota(jnp.int32, (PB, BK), 1))
-        & (col == 0)
-    )
-    g_ref[mine, :] += jnp.where(ridge, RIDGE, 0.0)
-    for c in started + scatter + spread + gram_copies:
-        c.wait_send()
+        if d == 1:
+            gram_send(3)
+            gram_send(4)
+        elif d == 3:
+            gram_relay(3)
+            gram_relay(4)
+
+    started += gather(turned, KEPT * BK, dag_send, dag_recv, while_spreading)
+    for i in range(NB):
+        for j in range(i + 1):
+            m = (j - i + KEPT - 1) % NB
+            if m < KEPT:
+                a_ref[i * BK : (i + 1) * BK, j * BK : (j + 1) * BK] = turned[i * BK : (i + 1) * BK, m * BK : (m + 1) * BK]
+            else:
+                m = (i - j + KEPT - 1) % NB
+                a_ref[i * BK : (i + 1) * BK, j * BK : (j + 1) * BK] = jnp.transpose(
+                    turned[j * BK : (j + 1) * BK, m * BK : (m + 1) * BK]
+                )
+
+    def sum_gram():
+        for c in gram_copies:
+            c.wait_recv()
+        for d in range(5):
+            ids = pieces(d)
+            for t in range(len(ids) // 2):
+                tile = first_tile[d] + t
+                total = gsend[tile, 0]
+                for s in range(len(direct)):
+                    total = total + grecv[tile, s]
+                total = jnp.transpose(total) * (1.0 / M)
+                for half in range(2):
+                    rows = pl.ds(pl.multiple_of(ids[2 * t + half] * 64, 64), 64)
+                    g_ref[rows, :] = total[half * 64 : half * 64 + 64, :]
+        ridge = (
+            (lax.broadcasted_iota(jnp.int32, (PB, BK), 0) == lax.broadcasted_iota(jnp.int32, (PB, BK), 1))
+            & (col == 0)
+        )
+        g_ref[mine, :] += jnp.where(ridge, RIDGE, 0.0)
 
     def out_copy(k, source):
         return pltpu.make_async_remote_copy(
@@ -368,7 +428,12 @@
         def _():
             out_copy(k, col).start()
 
-    factor_steps(a_ref, g_ref, diag, left_ref, right_ref, invl_ref, invr_ref, emit)
+    factor_steps(a_ref, g_ref, diag, left_ref, right_ref, invl_ref, invr_ref, sum_gram, emit)
+    for c in started + scatter + spread + gram_copies:
+        c.wait_send()
+    for pair in relays.values():
+        for c in pair:
+            c.wait_send()
     out_ref[:, here] = solved[here, :]
     for o in range(1, NB):
         k = col_peers[o - 1]
@@ -387,11 +452,13 @@
             pltpu.VMEM((1024, 2048), BF16),
             pltpu.VMEM((PANEL, 2048), BF16),
             pltpu.VMEM((PANEL, PANEL), F32),
+            pltpu.VMEM((PANEL, PANEL), F32),
             pltpu.VMEM((PB, PANEL), F32),
             pltpu.VMEM((NB, PB, BK), F32),
             pltpu.VMEM((PB, BK), F32),
             pltpu.VMEM((NB, NB, BK, BK), F32),
-            pltpu.VMEM((NB, NB, BK, BK), F32),
+            pltpu.VMEM((NB, 5, BK, BK), F32),
+            pltpu.VMEM((NB, 2, BK, BK), F32),
             pltpu.VMEM((PANEL, BK), F32),
             pltpu.VMEM((PANEL, BK), F32),
             pltpu.VMEM((BK, BK), F32),
@@ -399,7 +466,7 @@
             pltpu.VMEM((PANEL, 6 * BK), BF16),
             pltpu.VMEM((BK, 6 * BK), BF16),
             pltpu.VMEM((BK, 6 * BK), BF16),
-            sem((2,)), sem((33,)), sem((33,)), sem((33,)), sem((33,)),
+            sem((2,)), sem((16 + 17 * PARTS,)), sem((16 + 17 * PARTS,)), sem((16 + 17 * PARTS,)), sem((16 + 17 * PARTS,)),
             sem((NB,)), sem((NB,)), sem((NB,)), sem((NB,)),
             sem((5 * NB,)), sem((5 * NB,)), sem((NB,)), sem((NB,)),
         ],

time: 153 us -> 129 us (0.84)
  Pallas kernels: 151 us -> 126 us
    pallas_call x1, Pallas kernels: 151 us -> 126 us  [shards(): pl.pallas_call(kernel, out_shape=jax.ShapeDtypeStruct((BK, 1024), F32), i...]
where the time goes in v3:
time: 129 us; the launch traced here: 128 us
  Pallas kernels  126 us (98%)
  local copies, waits for them, and re-layouts  1.89 us (1%)
    pallas_call x1, Pallas kernels, shards(): pl.pallas_call(kernel, out_shape=jax.ShapeDtypeStruct((BK, 1024), F32), i...  126 us

profile of v3, /device:TPU:1, one launch (start us, length us, event | category | flops | bytes accessed | tf_op | source)
XLA Modules:
  0.0 128.4 jit_solution(15513052633078908707)
XLA Ops:
  0.0 126.5 %shard_map.17 = f32[128,1024]{1,0:T(8,128)} custom-call(bf16[1024,2048]{1,0:T(8,128)(2,1)} %markers_ref.1), custom_call_target="tpu_custom_call" | custom-call | tf_op jit(solution)/shard_map/pallas_call | solution.py:446
  126.5 1.9 %copy.3 = f32[128,1024]{1,0:T(8,128)} copy(f32[128,1024]{1,0:T(8,128)} %shard_map.17) | data formatting | bytes 1048576

commit v4 on v3

--- a/solution.py
+++ b/solution.py
@@ -80,11 +80,28 @@
     lane = lax.broadcasted_iota(jnp.int32, (8, BK), 1)
     sub = lax.broadcasted_iota(jnp.int32, (8, BK), 0)
     out = []
+    cols = [col_of(tiles[0], j) for j in range(8)]
     for t in range(16):
         x, b0 = tiles[t], 8 * t
-        cols = [col_of(x, b0 + j) for j in range(8)]
         w, rp = factor8([[row_of(cols[j], i) for j in range(i + 1)] for i in range(8)])
         inside = (lane >= b0) & (lane < b0 + 8)
+
+        def multipliers(i):
+            e = [col_of(tiles[i], b0 + j) for j in range(8)]
+            g = []
+            for s in range(8):
+                f = e[s]
+                for j in range(s):
+                    f = f + w[s][j] * e[j]
+                g.append(f)
+            return g
+
+        if t < 15:
+            g = multipliers(t + 1)
+            f = [g[s] * rp[s] for s in range(8)]
+            cols = [col_of(tiles[t + 1], b0 + 8 + j) for j in range(8)]
+            for s in range(8):
+                cols = [cols[j] - f[s] * row_of(g[s], j) for j in range(8)]
         xt = jnp.where(inside, (lane - b0 == sub).astype(F32), x)
         r = [row_of(xt, i) for i in range(8)]
         u = []
@@ -99,13 +116,11 @@
             p = jnp.where(sub == s, rp[s], p)
         out.append(jnp.where(lane <= b0 + sub, y * lax.sqrt(p), 0.0))
         for i in range(t + 1, 16):
-            e = [col_of(tiles[i], b0 + j) for j in range(8)]
+            if i > t + 1:
+                f = [h * q for h, q in zip(multipliers(i), rp)]
             z = jnp.where(inside, 0.0, tiles[i])
             for s in range(8):
-                f = e[s]
-                for j in range(s):
-                    f = f + w[s][j] * e[j]
-                z = z - (f * rp[s]) * u[s]
+                z = z - f[s] * u[s]
             tiles[i] = z
     return jnp.concatenate(out, axis=0)
 
@@ -115,30 +130,32 @@
 
 
 def factor_steps(a_ref, g_ref, diag, left_ref, right_ref, invl_ref, invr_ref, at_first, emit):
-    rows = lax.broadcasted_iota(jnp.int32, (PANEL, BK), 0)
     diag[...] = a_ref[:BK, :BK]
     invl_ref[...] = jnp.zeros_like(invl_ref)
     invr_ref[...] = jnp.zeros_like(invr_ref)
 
-    def step(k, carry):
+    def step(base, k, carry):
         here = block_at(k)
         before = block_at(jnp.maximum(k - 1, 0))
         after = block_at(jnp.minimum(k + 1, NB - 1))
         block = diag[...]
 
-        @pl.when(k == 1)
-        def _():
-            at_first()
+        if base == 0:
+            @pl.when(k == 1)
+            def _():
+                at_first()
 
         s_k = dot_nn(invl_ref[...], stack_right(g_ref[before, :], axis=0))
-        panel = dot_nt(stack_left(a_ref[:, before]), invr_ref[...])
+        panel = dot_nt(stack_left(a_ref[base:, before]), invr_ref[...])
+        rows = lax.broadcasted_iota(jnp.int32, (PANEL - base, BK), 0) + base
         panel = jnp.where(rows >= k * BK, panel, 0.0)
-        left_ref[...] = stack_left(panel)
-        right_ref[...] = stack_right(panel)
-        for j in range(NB // 2):
+        left_ref[base:, :] = stack_left(panel)
+        right_ref[base:, :] = stack_right(panel)
+        for j in range(base // (2 * BK), NB // 2):
             cols = slice(2 * BK * j, 2 * BK * (j + 1))
-            a_ref[:, cols] -= dot_nt(left_ref[...], right_ref[cols, :])
-        g_ref[...] -= dot_nn(left_ref[...], stack_right(s_k, axis=0))
+            top = 0 if j < NB // 4 else PANEL // 2
+            a_ref[top:, cols] -= dot_nt(left_ref[top:, :], right_ref[cols, :])
+        g_ref[base:, :] -= dot_nn(left_ref[base:, :], stack_right(s_k, axis=0))
         inverse = factor_inverse(block)
         inv_r = stack_right(inverse)
         invl_ref[...] = stack_left(inverse)
@@ -148,7 +165,8 @@
         emit(k - 1, s_k)
         return carry
 
-    lax.fori_loop(0, NB, step, 0)
+    lax.fori_loop(0, NB // 2, functools.partial(step, 0), 0)
+    lax.fori_loop(NB // 2, NB, functools.partial(step, PANEL // 2), 0)
     last = slice(PANEL - BK, PANEL)
     emit(NB - 1, dot_nn(invl_ref[...], stack_right(g_ref[last, :], axis=0)))
 
@@ -172,7 +190,9 @@
     partner = row_id(1 - hi, z, core)
     up = row_id(hi, lax.rem(z + 1, 8), core)
     down = row_id(hi, lax.rem(z + 7, 8), core)
-    row_peers = (sibling, partner, up, down)
+    up2 = row_id(hi, lax.rem(z + 2, 8), core)
+    down2 = row_id(hi, lax.rem(z + 6, 8), core)
+    row_peers = (sibling, partner, up, down, up2, down2)
     col_peers = [lax.rem(col + o, NB) for o in range(1, NB)]
 
     load_panel = pltpu.make_async_copy(
@@ -192,7 +212,7 @@
     def piece_id(h, zz):
         return h * 8 + zz
 
-    def gather(buf, width, send, recv, between):
+    def gather(buf, width, skip, send, recv, between):
         size = PB // PARTS
 
         def rows_of(r, part):
@@ -251,8 +271,11 @@
             for part in range(PARTS):
                 for stream, way in ways:
                     copy(source(stream, way, d), part, sibling, index_of(stream, way, d, part), go=False).wait_recv()
-                    if d < reach[stream, way]:
+                    if d < (min(3, reach[stream, way]) if skip else reach[stream, way]):
                         forward(stream, way, d, part)
+                    if skip and d == 2 and reach[stream, way] == 4:
+                        far = up2 if way == 0 else down2
+                        copy(source(stream, way, d), part, far, index_of(stream, way, 4, part))
             from_sibling()
             for stream, way in ways:
                 to_sibling(source(stream, way, d), n)
@@ -320,20 +343,20 @@
         for index in (3, 4):
             direct_copy(d, index)
 
-    a_ref[...] = jnp.zeros_like(a_ref)
-    g_ref[...] = jnp.zeros_like(g_ref)
     load_panel.wait()
 
     def while_gathering(d):
         if d == 1:
             load_own.wait()
+            a_ref[...] = jnp.zeros_like(a_ref)
+            g_ref[...] = jnp.zeros_like(g_ref)
         if d < 4:
             gram_chunk(d - 1)
             gram_send(d - 1)
         if d > 1:
             gram_relay(d - 2)
 
-    started = gather(panel, 2048, ag_send, ag_recv, while_gathering)
+    started = gather(panel, 2048, False, ag_send, ag_recv, while_gathering)
 
     mine = pl.ds(pl.multiple_of(row * PB, PB), PB)
     here = pl.ds(pl.multiple_of(col * BK, BK), BK)
@@ -383,7 +406,7 @@
             gram_relay(3)
             gram_relay(4)
 
-    started += gather(turned, KEPT * BK, dag_send, dag_recv, while_spreading)
+    started += gather(turned, KEPT * BK, True, dag_send, dag_recv, while_spreading)
     for i in range(NB):
         for j in range(i + 1):
             m = (j - i + KEPT - 1) % NB

time: 129 us -> 120 us (0.930)
  Pallas kernels: 126 us -> 118 us
    pallas_call x1, Pallas kernels: 126 us -> 118 us  [shards(): pl.pallas_call(kernel, out_shape=jax.ShapeDtypeStruct((BK, 1024), F32), i...]
where the time goes in v4:
time: 120 us
  Pallas kernels  118 us (98%)
  local copies, waits for them, and re-layouts  1.89 us (2%)
    pallas_call x1, Pallas kernels, shards(): pl.pallas_call(kernel, out_shape=jax.ShapeDtypeStruct((BK, 1024), F32), i...  118 us

profile of v4, /device:TPU:1, one launch (start us, length us, event | category | flops | bytes accessed | tf_op | source)
XLA Modules:
  0.0 119.8 jit_solution(14006445231692646881)
XLA Ops:
  0.0 117.9 %shard_map.17 = f32[128,1024]{1,0:T(8,128)} custom-call(bf16[1024,2048]{1,0:T(8,128)(2,1)} %markers_ref.1), custom_call_target="tpu_custom_call" | custom-call | tf_op jit(solution)/shard_map/pallas_call | solution.py:469
  117.9 1.9 %copy.3 = f32[128,1024]{1,0:T(8,128)} copy(f32[128,1024]{1,0:T(8,128)} %shard_map.17) | data formatting | bytes 1048576

commit v5 on v4

--- a/solution.py
+++ b/solution.py
@@ -79,10 +79,13 @@
     tiles = [a[8 * t : 8 * t + 8, :] for t in range(16)]
     lane = lax.broadcasted_iota(jnp.int32, (8, BK), 1)
     sub = lax.broadcasted_iota(jnp.int32, (8, BK), 0)
-    out = []
-    cols = [col_of(tiles[0], j) for j in range(8)]
+    out, scaled, plain = [], [], []
+    cols = None
     for t in range(16):
         x, b0 = tiles[t], 8 * t
+        end = 8 if t < 8 else 16
+        if cols is None:
+            cols = [col_of(x, b0 + j) for j in range(8)]
         w, rp = factor8([[row_of(cols[j], i) for j in range(i + 1)] for i in range(8)])
         inside = (lane >= b0) & (lane < b0 + 8)
 
@@ -96,7 +99,8 @@
                 g.append(f)
             return g
 
-        if t < 15:
+        cols = None
+        if t + 1 < end:
             g = multipliers(t + 1)
             f = [g[s] * rp[s] for s in range(8)]
             cols = [col_of(tiles[t + 1], b0 + 8 + j) for j in range(8)]
@@ -114,14 +118,26 @@
         for s in range(1, 8):
             y = jnp.where(sub == s, u[s], y)
             p = jnp.where(sub == s, rp[s], p)
-        out.append(jnp.where(lane <= b0 + sub, y * lax.sqrt(p), 0.0))
-        for i in range(t + 1, 16):
+        below = lane <= b0 + sub
+        out.append(jnp.where(below, y * lax.sqrt(p), 0.0))
+        for i in range(t + 1, end):
             if i > t + 1:
                 f = [h * q for h, q in zip(multipliers(i), rp)]
             z = jnp.where(inside, 0.0, tiles[i])
             for s in range(8):
                 z = z - f[s] * u[s]
             tiles[i] = z
+        if t < 8:
+            scaled.append(y * p)
+            plain.append(jnp.where(below | (lane >= 64), y, 0.0))
+        if t == 7:
+            lh, lm, ll = (x.astype(F32) for x in split3(jnp.concatenate(scaled, axis=0)))
+            rh, rm, rl = split3(jnp.concatenate(plain, axis=0))
+            half = jnp.where(lax.broadcasted_iota(jnp.int32, (64, BK), 1) < 64, 0.0, jnp.concatenate(tiles[8:], axis=0))
+            for left, right in (((lh, lm), (rl, rh)), ((lm, ll), (rm, rh)), ((lh, lh), (rh, rm))):
+                turned = jnp.transpose(jnp.concatenate(left, axis=0))[64:, :].astype(BF16)
+                half = half - dot_nn(turned, jnp.concatenate(right, axis=0))
+            tiles[8:] = [half[8 * i : 8 * i + 8, :] for i in range(8)]
     return jnp.concatenate(out, axis=0)
 
 
@@ -353,7 +369,7 @@
         if d < 4:
             gram_chunk(d - 1)
             gram_send(d - 1)
-        if d > 1:
+        if d in (2, 3):
             gram_relay(d - 2)
 
     started = gather(panel, 2048, False, ag_send, ag_recv, while_gathering)
@@ -402,6 +418,7 @@
         if d == 1:
             gram_send(3)
             gram_send(4)
+            gram_relay(2)
         elif d == 3:
             gram_relay(3)
             gram_relay(4)

time: 120 us -> 115 us (0.958)
  Pallas kernels: 118 us -> 113 us
    pallas_call x1, Pallas kernels: 118 us -> 113 us  [shards(): pl.pallas_call(kernel, out_shape=jax.ShapeDtypeStruct((BK, 1024), F32), i...]
where the time goes in v5:
time: 115 us
  Pallas kernels  113 us (98%)
  local copies, waits for them, and re-layouts  1.89 us (2%)
    pallas_call x1, Pallas kernels, shards(): pl.pallas_call(kernel, out_shape=jax.ShapeDtypeStruct((BK, 1024), F32), i...  113 us

profile of v5, /device:TPU:1, one launch (start us, length us, event | category | flops | bytes accessed | tf_op | source)
XLA Modules:
  0.0 114.6 jit_solution(6996258185244143667)
XLA Ops:
  0.0 112.7 %shard_map.17 = f32[128,1024]{1,0:T(8,128)} custom-call(bf16[1024,2048]{1,0:T(8,128)(2,1)} %markers_ref.1), custom_call_target="tpu_custom_call" | custom-call | tf_op jit(solution)/shard_map/pallas_call | solution.py:486
  112.7 1.9 %copy.3 = f32[128,1024]{1,0:T(8,128)} copy(f32[128,1024]{1,0:T(8,128)} %shard_map.17) | data formatting | bytes 1048576

commit v6 on v5

--- a/solution.py
+++ b/solution.py
@@ -309,7 +309,7 @@
         return [piece_id(hi, plus), piece_id(hi, minus), piece_id(1 - hi, plus), piece_id(1 - hi, minus)]
 
     first_tile = [0, 1, 3, 5, 7]
-    gram_copies = []
+    gram_copies = [[] for _ in range(5)]
 
     def col_at(dx, dy):
         return lax.rem(col // 2 + dx, 4) * 2 + lax.rem(col + dy, 2)
@@ -328,7 +328,7 @@
 
     def direct_copy(d, index):
         dx, dy = direct[index]
-        gram_copies.append(sums_copy(d, dx * 2 + dy, col_at(dx, dy), grecv, index, index))
+        gram_copies[d].append(sums_copy(d, dx * 2 + dy, col_at(dx, dy), grecv, index, index))
 
     relays = {}
 
@@ -371,12 +371,23 @@
             gram_send(d - 1)
         if d in (2, 3):
             gram_relay(d - 2)
-
-    started = gather(panel, 2048, False, ag_send, ag_recv, while_gathering)
+        if d == 4:
+            for o in (1, 2, 3):
+                for h in range(2):
+                    diagonal_part(h, o)
 
     mine = pl.ds(pl.multiple_of(row * PB, PB), PB)
     here = pl.ds(pl.multiple_of(col * BK, BK), BK)
-    dpart[...] = dot_nt(panel[mine, :], panel[...])
+
+    def diagonal_part(h, o):
+        tile = h * 4 + lax.rem(lax.rem(z + 4, 8) // 2 + o, 4)
+        cols = pl.ds(pl.multiple_of(tile * BK, BK), BK)
+        dpart[:, cols] = dot_nt(panel[mine, :], panel[cols, :])
+
+    started = gather(panel, 2048, False, ag_send, ag_recv, while_gathering)
+
+    for h in range(2):
+        diagonal_part(h, 0)
 
     def reduce_copy(o, target):
         return pltpu.make_async_remote_copy(
@@ -414,6 +425,20 @@
     for c in spread:
         c.wait_recv()
 
+    def sum_chunk(d):
+        for c in gram_copies[d]:
+            c.wait_recv()
+        ids = pieces(d)
+        for t in range(len(ids) // 2):
+            tile = first_tile[d] + t
+            total = gsend[tile, 0]
+            for s in range(len(direct)):
+                total = total + grecv[tile, s]
+            total = jnp.transpose(total) * (1.0 / M)
+            for half in range(2):
+                rows = pl.ds(pl.multiple_of(ids[2 * t + half] * 64, 64), 64)
+                g_ref[rows, :] = total[half * 64 : half * 64 + 64, :]
+
     def while_spreading(d):
         if d == 1:
             gram_send(3)
@@ -422,6 +447,9 @@
         elif d == 3:
             gram_relay(3)
             gram_relay(4)
+        elif d == 2:
+            sum_chunk(0)
+            sum_chunk(1)
 
     started += gather(turned, KEPT * BK, True, dag_send, dag_recv, while_spreading)
     for i in range(NB):
@@ -436,19 +464,8 @@
                 )
 
     def sum_gram():
-        for c in gram_copies:
-            c.wait_recv()
-        for d in range(5):
-            ids = pieces(d)
-            for t in range(len(ids) // 2):
-                tile = first_tile[d] + t
-                total = gsend[tile, 0]
-                for s in range(len(direct)):
-                    total = total + grecv[tile, s]
-                total = jnp.transpose(total) * (1.0 / M)
-                for half in range(2):
-                    rows = pl.ds(pl.multiple_of(ids[2 * t + half] * 64, 64), 64)
-                    g_ref[rows, :] = total[half * 64 : half * 64 + 64, :]
+        for d in (2, 3, 4):
+            sum_chunk(d)
         ridge = (
             (lax.broadcasted_iota(jnp.int32, (PB, BK), 0) == lax.broadcasted_iota(jnp.int32, (PB, BK), 1))
             & (col == 0)
@@ -469,7 +486,7 @@
             out_copy(k, col).start()
 
     factor_steps(a_ref, g_ref, diag, left_ref, right_ref, invl_ref, invr_ref, sum_gram, emit)
-    for c in started + scatter + spread + gram_copies:
+    for c in started + scatter + spread + sum(gram_copies, []):
         c.wait_send()
     for pair in relays.values():
         for c in pair:

time: 115 us -> 115 us (level)
  no operation moved by 1% of the time
where the time goes in v6:
time: 115 us
  Pallas kernels  113 us (98%)
  local copies, waits for them, and re-layouts  1.89 us (2%)
    pallas_call x1, Pallas kernels, shards(): pl.pallas_call(kernel, out_shape=jax.ShapeDtypeStruct((BK, 1024), F32), i...  113 us

profile of v6, /device:TPU:1, one launch (start us, length us, event | category | flops | bytes accessed | tf_op | source)
XLA Modules:
  0.0 114.8 jit_solution(4645594315017779589)
XLA Ops:
  0.0 112.9 %shard_map.17 = f32[128,1024]{1,0:T(8,128)} custom-call(bf16[1024,2048]{1,0:T(8,128)(2,1)} %markers_ref.1), custom_call_target="tpu_custom_call" | custom-call | tf_op jit(solution)/shard_map/pallas_call | solution.py:503
  112.9 1.9 %copy.3 = f32[128,1024]{1,0:T(8,128)} copy(f32[128,1024]{1,0:T(8,128)} %shard_map.17) | data formatting | bytes 1048576

commit v7 on v5

--- a/solution.py
+++ b/solution.py
@@ -474,11 +474,13 @@
     for pair in relays.values():
         for c in pair:
             c.wait_send()
-    out_ref[:, here] = solved[here, :]
+    keep = pltpu.make_async_copy(solved.at[here, :], out_ref.at[:, here], local_sem.at[0])
+    keep.start()
     for o in range(1, NB):
         k = col_peers[o - 1]
         out_copy(k, col).wait_send()
         out_copy(k, k).wait_recv()
+    keep.wait()
 
 
 def shards(markers):
@@ -487,7 +489,7 @@
         kernel,
         out_shape=jax.ShapeDtypeStruct((BK, 1024), F32),
         in_specs=[pl.BlockSpec(memory_space=pl.ANY)],
-        out_specs=pl.BlockSpec(memory_space=pltpu.VMEM),
+        out_specs=pl.BlockSpec(memory_space=pl.ANY),
         scratch_shapes=[
             pltpu.VMEM((1024, 2048), BF16),
             pltpu.VMEM((PANEL, 2048), BF16),

time: 115 us -> 114 us (level)
  no operation moved by 1% of the time
where the time goes in v7:
time: 114 us
  Pallas kernels  112 us (98%)
  local copies, waits for them, and re-layouts  1.89 us (2%)
    pallas_call x1, Pallas kernels, shards(): pl.pallas_call(kernel, out_shape=jax.ShapeDtypeStruct((BK, 1024), F32), i...  112 us

profile of v7, /device:TPU:1, one launch (start us, length us, event | category | flops | bytes accessed | tf_op | source)
XLA Modules:
  0.0 113.9 jit_solution(4372793257104475754)
XLA Ops:
  0.0 112.0 %shard_map.17 = f32[128,1024]{1,0:T(8,128)} custom-call(bf16[1024,2048]{1,0:T(8,128)(2,1)} %markers_ref.1), custom_call_target="tpu_custom_call" | custom-call | tf_op jit(solution)/shard_map/pallas_call | solution.py:488
  112.0 1.9 %copy.3 = f32[128,1024]{1,0:T(8,128)} copy(f32[128,1024]{1,0:T(8,128)} %shard_map.17) | data formatting | bytes 1048576
